TPU v7x, 256 devices: a whole 4x4x8 slice. The times are simulated.
256 devices in a mesh: dp: 16 (over x, y), tensor: 16 (over z, core).
Axes of the slice: x: 4, y: 4, z: 8, core: 2. Of those that a mesh axis runs over, the one named last changes fastest.
Arguments:
- inputs: bfloat16 [16384, 8192], P('dp', 'tensor'), may hold values from -6 to 6
- output_gradient: bfloat16 [16384, 8192], P(('dp', 'tensor')), may hold values from -6 to 6
- weight: bfloat16 [8192, 8192], P('tensor'), may hold values from -0.0625 to 0.0625
- adapter_down: bfloat16 [32, 64, 8192], P('dp', None, 'tensor'), may hold values from -0.0625 to 0.0625
- adapter_up: bfloat16 [32, 64, 8192], P('dp', None, 'tensor'), may hold values from -0.0625 to 0.0625
- segment_adapter: int32 [128], replicated, may hold values from 0 to 31, as said below
- adapter_slot_map: int32 [32], replicated, may hold values from 0 to 31, as said below
Outputs:
- input_gradient: bfloat16 [16384, 8192], P('dp', 'tensor')
- grad_down: float32 [32, 64, 8192], P('dp', None, 'tensor')
- grad_up: float32 [32, 64, 8192], P('dp', None, 'tensor')
Inputs may be any that keep to these rules, and one draw needn't show every extreme that they name: `segment_adapter`: the adapter of slot j is stored on dp index j // 2. The segments of one replica use adapters of exactly 4 dp indices, 2 segments each. `adapter_slot_map`: A permutation of the adapters.
All inputs are finite; a program needn't handle non-finite values.
Results may differ from a plain program's by a relative error of at most 0.0029.
Values may be sent and summed in bfloat16 or wider, within the bound.
A program may use at most 128 MiB of HBM per device.

v0:
```python
import jax
import jax.numpy as jnp
from jax import lax
from jax.sharding import PartitionSpec as P

SEGMENT_TOKENS = 128


ADAPTER_SCALE = 0.5


def on_device(
    inputs, output_gradient, weight, adapter_down, adapter_up, segment_adapter, adapter_slot_map
):
    n_dp = lax.axis_size("dp")
    replica = lax.axis_index("dp")
    tensor_pos = lax.axis_index("tensor")
    tok_rows = inputs.shape[0]
    local_width = inputs.shape[1]
    rank_extent = adapter_down.shape[1]
    holding_count = adapter_down.shape[0]
    total_adapters = adapter_slot_map.shape[0]
    seg_count = tok_rows // SEGMENT_TOKENS
    capacity = max(2, seg_count // n_dp)
    adapter_ids = jnp.arange(total_adapters, dtype=jnp.int32)
    all_ids = segment_adapter.reshape(n_dp, seg_count)
    slot_table = jnp.sum(jnp.where(all_ids[:, :, None] == adapter_ids, adapter_slot_map, 0), axis=2)
    owner_rows = slot_table // holding_count
    within_owner = slot_table % holding_count
    earlier = jnp.arange(seg_count)[:, None] > jnp.arange(seg_count)[None, :]
    same_owner = owner_rows[:, :, None] == owner_rows[:, None, :]
    rank_rows = jnp.sum(jnp.where(same_owner & earlier[None], 1, 0), axis=2)
    replica_rows = jnp.arange(n_dp) == replica
    my_owner = jnp.sum(jnp.where(replica_rows[:, None], owner_rows, 0), axis=0)
    my_rank = jnp.sum(jnp.where(replica_rows[:, None], rank_rows, 0), axis=0)
    my_slots = jnp.sum(jnp.where(replica_rows[:, None], slot_table, 0), axis=0)
    owner_ids = jnp.arange(n_dp)
    slot_ids = jnp.arange(capacity)
    local_ids = jnp.arange(holding_count)
    send_pick = (
        (owner_rows == replica)[:, :, None, None]
        & (rank_rows[:, :, None, None] == slot_ids[:, None])
        & (within_owner[:, :, None, None] == local_ids)
    )
    outgoing = jnp.sum(send_pick.astype(jnp.float32), axis=1)
    stacked_factors = jnp.concatenate([adapter_down, adapter_up], axis=1)
    sending = jnp.einsum(
        "rkj,jcd->rkcd",
        outgoing.astype(jnp.bfloat16),
        stacked_factors,
        preferred_element_type=jnp.float32,
    ).astype(jnp.bfloat16)
    arrived = lax.all_to_all(sending, "dp", split_axis=0, concat_axis=0, tiled=True)
    take_pick = (
        (my_owner[:, None, None] == owner_ids[:, None]) & (my_rank[:, None, None] == slot_ids)
    ).astype(jnp.float32)
    seg_blocks = jnp.einsum(
        "sok,okcd->scd", take_pick.astype(jnp.bfloat16), arrived, preferred_element_type=jnp.float32
    ).astype(jnp.bfloat16)
    segment_down = seg_blocks[:, :rank_extent]
    segment_up = seg_blocks[:, rank_extent:]
    full_grad = lax.all_gather(output_gradient, "tensor", axis=0, tiled=True)
    own_columns = lax.dynamic_slice_in_dim(full_grad, tensor_pos * local_width, local_width, 1)
    own_columns = own_columns.reshape(seg_count, SEGMENT_TOKENS, local_width)
    seg_inputs = inputs.reshape(seg_count, SEGMENT_TOKENS, local_width)
    down_part = jnp.einsum(
        "sxc,src->sxr", seg_inputs, segment_down, preferred_element_type=jnp.float32
    )
    up_part = jnp.einsum(
        "sxc,src->sxr", own_columns, segment_up, preferred_element_type=jnp.float32
    )
    down_acts, up_grads = lax.psum((down_part, up_part), "tensor")
    down_bf = down_acts.astype(jnp.bfloat16)
    up_halfwidth = up_grads.astype(jnp.bfloat16)
    frozen_term = lax.dot_general(
        full_grad, weight, (((1,), (1,)), ((), ())), preferred_element_type=jnp.float32
    )
    adapter_term = jnp.einsum(
        "sxr,src->sxc", up_halfwidth, segment_down, preferred_element_type=jnp.float32
    ).reshape(tok_rows, local_width)
    projected_gradient = (frozen_term + ADAPTER_SCALE * adapter_term).astype(jnp.bfloat16)
    gradient_scale = ADAPTER_SCALE / SEGMENT_TOKENS
    seg_down = gradient_scale * jnp.einsum(
        "sxr,sxc->src", up_halfwidth, seg_inputs, preferred_element_type=jnp.float32
    )
    seg_up = gradient_scale * jnp.einsum(
        "sxr,sxc->src", down_bf, own_columns, preferred_element_type=jnp.float32
    )
    seg_terms = jnp.concatenate([seg_down, seg_up], axis=1)
    onehot = (my_slots[:, None] == adapter_ids).astype(jnp.float32)
    full_table = jnp.einsum("sa,scd->acd", onehot, seg_terms, precision=lax.Precision.HIGHEST)
    owned_grads = lax.psum_scatter(full_table, "dp", scatter_dimension=0, tiled=True)
    return (projected_gradient, owned_grads[:, :rank_extent], owned_grads[:, rank_extent:])


def solution(mesh):
    in_specs = (
        P("dp", "tensor"),
        P(("dp", "tensor"), None),
        P("tensor", None),
        P("dp", None, "tensor"),
        P("dp", None, "tensor"),
        P(),
        P(),
    )
    out_specs = (P("dp", "tensor"), P("dp", None, "tensor"), P("dp", None, "tensor"))
    return jax.shard_map(
        on_device, mesh=mesh, in_specs=in_specs, out_specs=out_specs, check_vma=False
    )
```

profile of v0, /device:TPU:1, one launch (start us, length us, event | category | flops | bytes accessed | tf_op | source)
XLA Modules:
  0.0 275.0 jit_solution(7088739767921542732)
XLA Ops:
  7.2 0.0 copy-start
  7.2 0.0 all-gather.2.cloned.1.call-start
  7.2 0.7 all-gather.2.cloned.1.call-update
  7.9 1.0 copy.49
  9.0 1.0 copy.48
  10.0 0.7 eq.137
  10.7 1.1 select_reduce_fusion
  11.8 0.1 copy.44
  11.9 0.1 select_reduce_fusion.1
  12.0 0.1 select_reduce_fusion.2
  12.2 1.7 convolution_convert_fusion
  13.9 6.3 %copy.50 = bf16[16,2,128,512]{3,1,2,0:T(2,128)(2,1)} copy(bf16[16,2,128,512]{3,0,1,2:T(8,128)(2,1)S(1)} %convolution_convert_fusion) | data formatting | bytes 8388608 | tf_op jit(solution)/shard_map/convert_element_type | solution.py:52
  20.2 7.6 %all-to-all-start = ((bf16[16,2,128,512]{3,1,2,0:T(2,128)(2,1)}), bf16[16,2,128,512]{3,1,2,0:T(2,128)(2,1)}, u32[]{:S(2)}, u32[]{:S(2)}) async-start(bf16[16,2,128,512]{3,1,2,0:T(2,128)(2,1)} %copy.50), calls=%async_computation | async-start | bytes 8388608 | tf_op jit(solution)/shard_map/all_to_all | solution.py:53
  27.8 0.0 reduce-scatter.2.cloned.1.call-start
  27.9 0.1 iota_compare_fusion.5
  27.9 60.9 %all-to-all-done = bf16[16,2,128,512]{3,1,2,0:T(2,128)(2,1)} async-done(((bf16[16,2,128,512]{3,1,2,0:T(2,128)(2,1)}), bf16[16,2,128,512]{3,1,2,0:T(2,128)(2,1)}, u32[]{:S(2)}, u32[]{:S(2)}) %all-to-all-start) | async-done | bytes 4194336 | tf_op jit(solution)/shard_map/all_to_all | solution.py:53
  88.9 4.6 %bitcast_convert_fusion = bf16[8,128,512]{2,0,1:T(8,128)(2,1)S(1)} fusion(bf16[16,2,128,512]{3,1,2,0:T(2,128)(2,1)} %all-to-all-done, pred[8,2]{0,1:T(4,128)(4,1)S(1)} %iota_compare_fusion.6, pred[8,16]{1,0:T(8,128)(4,1)S(1)} %iota_compare_fusion.5), kind=kOutput, calls=%fused_computation.6 | convolution fusion | flops 34079488 | bytes 5243024 | tf_op jit(solution)/shard_map/sok,okcd->scd/dot_general | solution.py:57
  93.5 0.1 fusion.29
  93.6 0.0 copy-done
  93.6 0.5 convolution_bitcast_fusion
  94.1 15.4 %all-gather.2.cloned.1.call-done = bf16[1024,8192]{1,0:T(8,128)(2,1)} async-done(((bf16[64,8192]{1,0:T(8,128)(2,1)}), bf16[1024,8192]{1,0:T(8,128)(2,1)}) %all-gather.2.cloned.1.call-update) | async-done | bytes 16777232 | tf_op jit(solution)/shard_map/all_gather | solution.py:62
  109.5 1.3 constant_dynamic-slice_fusion
  110.8 1.2 fusion.7
  112.0 48.9 %all-reduce.2 = (bf16[8,128,64]{1,2,0:T(8,128)(2,1)S(1)}, bf16[8,128,64]{1,2,0:T(8,128)(2,1)S(1)}) all-reduce(f32[8,128,64]{1,2,0:T(8,128)} %fusion.7, f32[8,128,64]{1,2,0:T(8,128)S(1)} %convolution_bitcast_fusion), channel_id=1, replica_groups=mesh['dp'=16,'tensor'=16] {'tensor'}, use_global_device_ids=true, to_apply=%region_5.6 | all-reduce | flops 131072 | bytes 786432 | tf_op jit(solution)/shard_map/psum | solution.py:72
  160.9 0.3 convolution_multiply_fusion.1
  161.2 0.3 convolution_multiply_fusion.2
  161.5 0.3 pad_maximum_fusion
  161.8 4.0 %fusion.3 = f32[32,128,512]{2,0,1:T(8,128)S(1)} fusion(f32[8,128,512]{2,1,0:T(8,128)S(1)} %pad_maximum_fusion, s32[8]{0:T(128)S(1)} %get-tuple-element.9), kind=kOutput, calls=%fused_computation.7 | convolution fusion | flops 201326848 | bytes 10485792 | tf_op jit(solution)/shard_map/sa,scd->acd/dot_general | solution.py:91
  165.8 8.1 %copy.57 = f32[32,128,512]{2,1,0:T(8,128)} copy(f32[32,128,512]{2,0,1:T(8,128)S(1)} %fusion.3) | data formatting | bytes 16777216 | tf_op jit(solution)/shard_map/sa,scd->acd/dot_general | solution.py:91
  173.9 0.0 reduce-scatter.2.cloned.1.call-update
  173.9 0.5 convolution_multiply_fusion
  174.4 0.0 copy-start.1
  174.5 15.9 %fusion.2 = bf16[1024,512]{1,0:T(8,128)(2,1)} fusion(f32[8,128,512]{2,1,0:T(8,128)S(1)} %convolution_multiply_fusion, bf16[1024,8192]{1,0:T(8,128)(2,1)} %all-gather.2.cloned.1.call-done, bf16[512,8192]{1,0:T(8,128)(2,1)} %param.9), kind=kOutput, calls=%fused_computation.5 | convolution fusion | flops 8590983168 | bytes 28311552 | tf_op jit(solution)/shard_map/dot_general | solution.py:75
  190.4 75.9 %reduce-scatter.2.cloned.1.call-done = f32[2,128,512]{2,1,0:T(8,128)} async-done(((f32[32,128,512]{2,1,0:T(8,128)}), f32[2,128,512]{2,1,0:T(8,128)}) %reduce-scatter.2.cloned.1.call-update) | async-done | bytes 524304 | tf_op jit(solution)/shard_map/reduce_scatter | solution.py:92
  266.3 1.9 fusion.30
  268.1 0.0 copy-done.1
  (6 shorter events, 0.1 us)
Async XLA Ops:
  7.2 86.4 %copy-start = (bf16[1024,512]{1,0:T(8,128)(2,1)S(1)}, bf16[1024,512]{1,0:T(8,128)(2,1)}, u32[]{:S(2)}) copy-start(bf16[1024,512]{1,0:T(8,128)(2,1)} %param.7) | copy-start | bytes 3145732
  7.2 102.3 %all-gather.2.cloned.1.call-start = ((), (), s32[]{:S(2)}) async-start(), calls=%async_computation.2 | async-start | bytes 17825792 | tf_op jit(solution)/shard_map/all_gather | solution.py:62
  20.2 68.7 %all-to-all-start = ((bf16[16,2,128,512]{3,1,2,0:T(2,128)(2,1)}), bf16[16,2,128,512]{3,1,2,0:T(2,128)(2,1)}, u32[]{:S(2)}, u32[]{:S(2)}) async-start(bf16[16,2,128,512]{3,1,2,0:T(2,128)(2,1)} %copy.50), calls=%async_computation | async-start | bytes 8388608 | tf_op jit(solution)/shard_map/all_to_all | solution.py:53
  27.8 238.5 %reduce-scatter.2.cloned.1.call-start = ((), (), s32[]{:S(2)}) async-start(), calls=%async_computation.3 | async-start | bytes 8912896 | tf_op jit(solution)/shard_map/reduce_scatter | solution.py:92
  174.4 93.7 %copy-start.1 = (bf16[1024,512]{1,0:T(8,128)(2,1)S(1)}, bf16[1024,512]{1,0:T(8,128)(2,1)}, u32[]{:S(2)}) copy-start(bf16[1024,512]{1,0:T(8,128)(2,1)} %param.7) | copy-start | bytes 3145732
Sparse Core Ops, SparseCore 0:
  9.8 99.6 all-gather.1
  174.0 92.1 reduce-scatter.1
where the time goes:
time: 276 us; the launch traced here: 275 us
  waiting for transfers between devices  153 us (55%)
  blocking collectives  48.9 us (18%)
  matrix products  29 us (11%)
  local copies, waits for them, and re-layouts  20.5 us (7%)
  between operations  14.2 us (5%)
  starting transfers between devices  7.71 us (3%)
    reduce_scatter x1, waiting for transfers between devices, on_device(): lax.psum_scatter(full_table, 'dp', scatter_dimension=0, tiled=True)  75.9 us
    all_to_all x1, waiting for transfers between devices, on_device(): lax.all_to_all(sending, 'dp', split_axis=0, concat_axis=0, tiled=True)  60.9 us
    psum x1, blocking collectives, on_device(): down_acts, up_grads = lax.psum((down_part, up_part), 'tensor')  48.9 us
    dot_general x1, matrix products, on_device(): lax.dot_general(full_grad, weight, (((1,), (1,)), ((), ())), preferred_el...  15.9 us
    all_gather x1, waiting for transfers between devices, on_device(): full_grad = lax.all_gather(output_gradient, 'tensor', axis=0, tiled=True)  15.4 us
    dot_general x1, local copies, waits for them, and re-layouts, on_device(): jnp.einsum('sa,scd->acd', onehot, seg_terms, precision=lax.Precision.HIGH...  8.08 us
    all_to_all x1, starting transfers between devices, on_device(): lax.all_to_all(sending, 'dp', split_axis=0, concat_axis=0, tiled=True)  7.63 us
    convert_element_type x1, local copies, waits for them, and re-layouts, on_device(): sending = jnp.einsum('rkj,jcd->rkcd', outgoing.astype(jnp.bfloat16), stac...  6.28 us
  transfers between devices with their start and end apart: 3, of which 3 were waited for; matrix products, arithmetic and copies ran while one was open for 12% of the time, Pallas kernels for 0%

commit v1 on v0

v1 whole, which is shorter than its diff:
```python
import functools

import jax
import jax.numpy as jnp
from jax import lax
from jax.experimental import pallas as pl
from jax.experimental.pallas import tpu as pltpu
from jax.sharding import PartitionSpec as P

MESH = pl.DeviceIdType.MESH
SCALE = 0.5
SEG = 128
NZ = 8
RANK = 64
HALF = 32
NT = (((1,), (1,)), ((), ()))
TN = (((0,), (0,)), ((), ()))
NN = (((1,), (0,)), ((), ()))

FIRST = [(4, 0), (3, 0), (4, 1), (2, 0), (3, 1), (4, 2), (1, 0), (2, 1), (3, 2), (4, 3)]
SECOND = [(r, a) for a in range(3) for r in range(a, -4, -1)] + [(3, 3), (2, 3), (1, 3), (0, 3)]
ROUNDS = FIRST + SECOND
LAST = len(ROUNDS) - 1


def dot(a, b, dims):
    return lax.dot_general(a, b, dims, preferred_element_type=jnp.float32)


def kernel(
    seg_ref, map_ref, x_hbm, g_hbm, w_hbm, fd_hbm, fu_hbm,
    out_ref, gd_ref, gu_ref,
    grads, weight, acts_in, fd, fu, acc,
    part, part_in, chip_part, rank_in, acts, lhs,
    tab0, tab1, tin0, tin1, sum0, sum1, sin0, sin1,
    loc, zr, dr, zs, ds, fr, fs, pr, ps, tr, ts,
):
    dp = lax.axis_index("dp")
    tp = lax.axis_index("tensor")
    z, c = tp // 2, tp % 2
    x, y = dp // 4, dp % 4
    partner = (dp, z * 2 + (1 - c))

    def at_z(zz):
        return (dp, (zz % NZ) * 2 + c)

    def at_x(xx):
        return ((xx % 4) * 4 + y, tp)

    def at_y(yy):
        return (x * 4 + yy % 4, tp)

    def remote(src, dst, send, recv, device):
        return pltpu.make_async_remote_copy(
            src_ref=src, dst_ref=dst, send_sem=send, recv_sem=recv,
            device_id=device, device_id_type=MESH,
        )

    own = []
    for j in range(NZ):
        own.append(pltpu.make_async_copy(
            g_hbm.at[:, pl.ds(j * 1024, 1024)], grads.at[(j * NZ + z) * 2 + c], loc.at[j]))
    own_fd = pltpu.make_async_copy(fd_hbm, fd.at[pl.ds((x * 4 + y) * 2, 2)], loc.at[8])
    own_fu = pltpu.make_async_copy(fu_hbm, fu.at[pl.ds((y * 4 + x) * 2, 2)], loc.at[9])
    load_x = pltpu.make_async_copy(x_hbm, acts_in, loc.at[10])
    load_w = [
        pltpu.make_async_copy(w_hbm.at[:, pl.ds(j * 1024, 1024)], weight.at[j], loc.at[11 + j])
        for j in range(NZ)
    ]
    for cp in own + [own_fd, own_fu, load_x] + load_w:
        cp.start()

    barrier = pltpu.get_barrier_semaphore()
    for d in range(1, NZ):
        pl.semaphore_signal(barrier, inc=1, device_id=at_z(z + d), device_id_type=MESH)
    for d in range(1, 4):
        pl.semaphore_signal(barrier, inc=1, device_id=at_x(x + d), device_id_type=MESH)
        pl.semaphore_signal(barrier, inc=1, device_id=at_y(y + d), device_id_type=MESH)
    pl.semaphore_signal(barrier, inc=1, device_id=partner, device_id_type=MESH)
    pl.semaphore_wait(barrier, 14)

    def zcopy(s, j, zz):
        i = (j * NZ + s) * 2 + c
        return remote(grads.at[i], grads.at[i], zs, zr.at[j * NZ + s], at_z(zz))

    def dcopy(s, j, core):
        i = (j * NZ + s) * 2 + core
        return remote(grads.at[i], grads.at[i], ds, dr.at[j * NZ + s], partner)

    def chunk(way, r, a):
        s = (z - way * a + 2 * NZ) % NZ
        return s, (s + way * r + 2 * NZ) % NZ

    def issue(k):
        r, a = ROUNDS[k]
        if a == 3 and r in (0, 4):
            @pl.when(c == 0)
            def _():
                zcopy(*chunk(1, r, a), z + 1).start()

            @pl.when(c == 1)
            def _():
                zcopy(*chunk(-1, r, a), z + NZ - 1).start()
        else:
            zcopy(*chunk(1, r, a), z + 1).start()
            zcopy(*chunk(-1, r, a), z + NZ - 1).start()

    def retire(k):
        r, a = ROUNDS[k]
        ways = (1,) if a == 3 and r in (0, 4) else (1, -1)
        for way in ways:
            s, j = chunk(way, r, a + 1)
            zcopy(s, j, z + 1).wait_recv()
            dcopy(s, j, c).start()

    def frozen(s, first, count, order):
        def body(n, carry):
            j = order(n)
            dcopy(s, j, 1 - c).wait_recv()
            g = grads[pl.ds((j * NZ + s) * 2, 2)].reshape(SEG, 1024)
            acc[s] += dot(g, weight[j], NT)
            return carry
        lax.fori_loop(first, first + count, body, 0)

    def slot_of(s):
        return map_ref[seg_ref[dp * NZ + s]]

    def finish(s):
        slot = slot_of(s)
        act = acts[1, pl.ds(0, 2), s].reshape(RANK, SEG)
        out = acc[s] + SCALE * dot(act, fd[slot], TN)
        out_ref[pl.ds(pl.multiple_of(s * SEG, SEG), SEG), :] = out.astype(jnp.bfloat16)

    kinds = ((fd, at_y, y, at_x, x), (fu, at_x, x, at_y, y))

    def factors_first(q):
        buf, at1, p1, _, p2 = kinds[q]
        mine = pl.ds((p2 * 4 + p1) * 2, 2)
        return [remote(buf.at[mine], buf.at[mine], fs.at[q], fr.at[q, d - 1], at1(p1 + d)) for d in (1, 2, 3)]

    def factors_second(q):
        buf, _, _, at2, p2 = kinds[q]
        rows = pl.ds(p2 * 8, 8)
        return [remote(buf.at[rows], buf.at[rows], fs.at[q], fr.at[q, 3], at2(p2 + 1)),
                remote(buf.at[rows], buf.at[rows], fs.at[q], fr.at[q, 4], at2(p2 + 3))]

    def factors_third(q):
        buf, _, _, at2, p2 = kinds[q]
        low = pl.ds(((p2 + 3) % 4) * 8, 4)
        high = pl.ds(((p2 + 1) % 4) * 8 + 4, 4)
        return [remote(buf.at[low], buf.at[low], fs.at[q], fr.at[q, 5], at2(p2 + 1)),
                remote(buf.at[high], buf.at[high], fs.at[q], fr.at[q, 6], at2(p2 + 3))]

    def start_all(copies):
        for cp in copies:
            cp.start()

    def await_all(copies):
        for cp in copies:
            cp.wait_recv()

    def project(q):
        def body(s, carry):
            slot = slot_of(s)
            if q == 0:
                t = dot(fd[slot], acts_in[pl.ds(pl.multiple_of(s * SEG, SEG), SEG), :], NT)
            else:
                owner = slot // 2
                row = ((owner % 4) * 4 + owner // 4) * 2 + slot % 2
                cols = pl.ds(pl.multiple_of(c * 512, 512), 512)
                g = grads[pl.ds((z * NZ + s) * 2, 2), :, cols].reshape(SEG, 512)
                t = dot(fu[row], g, NT)
            part[q, 0, s] = t[:HALF]
            part[q, 1, s] = t[HALF:]
            return carry
        lax.fori_loop(0, NZ, body, 0)

    def share_core(q):
        return remote(part.at[q, 1 - c], part_in.at[q], ps.at[q, 0], pr.at[q, 0], partner)

    def share_chips(q):
        return [remote(chip_part.at[q, (z + d) % NZ], rank_in.at[q, d - 1], ps.at[q, 1], pr.at[q, d], at_z(z + d))
                for d in range(1, NZ)]

    def share_acts(q):
        return [remote(acts.at[q, c, z], acts.at[q, c, z], ps.at[q, 2], pr.at[q, 7 + d], at_z(z + d))
                for d in range(1, NZ)]

    def await_acts(q):
        for d in range(1, NZ):
            s = (z + NZ - d) % NZ
            remote(acts.at[q, c, s], acts.at[q, c, s], ps.at[q, 2], pr.at[q, 7 + d], at_z(z + d)).wait_recv()

    def cross_acts(q):
        return remote(acts.at[q, c], acts.at[q, c], ps.at[q, 3], pr.at[q, 15], partner)

    def await_cross(q):
        remote(acts.at[q, 1 - c], acts.at[q, 1 - c], ps.at[q, 3], pr.at[q, 15], partner).wait_recv()

    def reduce_core(q):
        share_core(q).wait_recv()
        chip_part[q] = part[q, c] + part_in[q]
        start_all(share_chips(q))

    def reduce_chips(q):
        await_all(share_chips(q))
        t = chip_part[q, z]
        for d in range(NZ - 1):
            t = t + rank_in[q, d]
        acts[q, c, z] = t.astype(jnp.bfloat16)
        start_all(share_acts(q))

    routes = ((tab0, tin0, sum0, sin0, at_x, x, at_y, y), (tab1, tin1, sum1, sin1, at_y, y, at_x, x))

    def table(q):
        for h in range(2):
            tab = routes[h][0]

            def body(g, carry):
                for s in range(NZ):
                    slot = slot_of(s)
                    v = acts[q, h, s]
                    for i in range(8):
                        a = g * 8 + i if h == 0 else (i // 2) * 8 + g * 2 + i % 2
                        lhs[i * HALF:(i + 1) * HALF, s * SEG:(s + 1) * SEG] = jnp.where(
                            slot == a, v, jnp.zeros_like(v))
                if q == 0:
                    cols = pl.ds(pl.multiple_of(c * 512, 512), 512)
                    rhs = grads[pl.ds(z * NZ * 2, NZ * 2), :, cols].reshape(NZ * SEG, 512)
                else:
                    rhs = acts_in[...]
                t = dot(lhs[...], rhs, NN) * (SCALE / SEG)
                tab[q, g] = t.astype(jnp.bfloat16).reshape(8, HALF, 512)
                return carry
            lax.fori_loop(0, 4, body, 0)
            start_all(table_first(q, h))

    def table_first(q, h):
        tab, tin, _, _, at1, p1, _, _ = routes[h]
        return [remote(tab.at[q, (p1 + d) % 4], tin.at[q, d - 1], ts.at[q, h, 0], tr.at[q, h, d - 1], at1(p1 + d))
                for d in (1, 2, 3)]

    def table_second(q, h):
        _, _, total, sin, _, _, at2, p2 = routes[h]
        return [remote(total.at[q, (p2 + d) % 4], sin.at[q, d - 1], ts.at[q, h, 1], tr.at[q, h, 2 + d], at2(p2 + d))
                for d in (1, 2, 3)]

    def table_sum(q):
        for h in range(2):
            tab, tin, total, _, _, p1, _, _ = routes[h]
            await_all(table_first(q, h))

            def body(n, carry):
                t = tab[q, p1, pl.ds(n * 2, 2)].astype(jnp.float32)
                for d in range(3):
                    t = t + tin[q, d, pl.ds(n * 2, 2)].astype(jnp.float32)
                total[q, n] = t
                return carry
            lax.fori_loop(0, 4, body, 0)
            start_all(table_second(q, h))

    def table_end(q):
        ref = (gu_ref, gd_ref)[q]
        for h in range(2):
            _, _, total, sin, _, _, _, p2 = routes[h]
            await_all(table_second(q, h))
            t = total[q, p2]
            for d in range(3):
                t = t + sin[q, d]
            ref[:, h * HALF:(h + 1) * HALF, :] = t

    def start_own():
        for j in range(NZ):
            dcopy(z, j, c).start()

    def zero():
        acc[...] = jnp.zeros_like(acc)

    def loads_done():
        load_x.wait()
        for cp in load_w:
            cp.wait()

    def forward(s):
        return lambda n: (s + n) % NZ

    def whole(s):
        frozen(s, 0, NZ, forward(s))

    def near(a, way):
        return (z + way * a + NZ) % NZ

    hooks = {
        0: [lambda: own_fd.wait(), lambda: own_fu.wait(), lambda: start_all(factors_first(0)),
            lambda: start_all(factors_first(1)), start_own],
        1: [zero],
        2: [lambda: await_all(factors_first(0)), lambda: await_all(factors_first(1)),
            lambda: start_all(factors_second(0)), lambda: start_all(factors_second(1))],
        3: [loads_done, lambda: whole(z)],
        6: [lambda: await_all(factors_second(0)), lambda: await_all(factors_second(1)),
            lambda: start_all(factors_third(0)), lambda: start_all(factors_third(1))],
        9: [lambda: await_all(factors_third(0)), lambda: project(0), lambda: share_core(0).start()],
        10: [lambda: await_all(factors_third(1)), lambda: reduce_core(0)],
        12: [lambda: own_cols_ready(), lambda: project(1), lambda: share_core(1).start(),
             lambda: reduce_chips(0)],
        13: [lambda: reduce_core(1)],
        14: [lambda: await_acts(0), lambda: cross_acts(0).start()],
        15: [lambda: await_cross(0), lambda: table(0), lambda: reduce_chips(1)],
        17: [lambda: await_acts(1), lambda: cross_acts(1).start(), lambda: frozen_rest(near(1, -1))],
        18: [lambda: await_cross(1), lambda: table(1)],
        19: [lambda: frozen_rest(near(1, 1))],
        20: [lambda: table_sum(0)],
        21: [lambda: finish(z), lambda: finish(near(1, -1)), lambda: finish(near(1, 1))],
        22: [lambda: frozen_rest(near(2, -1))],
        23: [lambda: frozen_rest(near(2, 1))],
        24: [lambda: table_end(0), lambda: table_sum(1)],
        25: [lambda: finish(near(2, -1)), lambda: finish(near(2, 1))],
        28: [lambda: frozen_rest(near(3, -1)), lambda: frozen_rest(near(3, 1)),
             lambda: finish(near(3, -1)), lambda: finish(near(3, 1)), lambda: table_end(1)],
    }

    def own_cols_ready():
        def body(n, carry):
            dcopy((z + n) % NZ, z, 1 - c).wait_recv()
            return carry
        lax.fori_loop(1, NZ, body, 0)

    def frozen_chunk(s, j):
        g = grads[pl.ds((j * NZ + s) * 2, 2)].reshape(SEG, 1024)
        acc[s] += dot(g, weight[j], NT)

    def frozen_rest(s):
        def body(n, carry):
            j = (z + n) % NZ
            dcopy(s, j, 1 - c).wait_recv()
            frozen_chunk(s, j)
            return carry
        frozen_chunk(s, z)
        lax.fori_loop(1, NZ, body, 0)

    for cp in own:
        cp.wait()
    done = 0
    for k in range(len(ROUNDS)):
        lag = 2 if k < len(FIRST) + 2 else 3
        while done <= k - lag:
            retire(done)
            done += 1
        issue(k)
        for hook in hooks.get(k, []):
            hook()
    far = near(4, 1)
    while done < LAST:
        retire(done)
        done += 1

    frozen_chunk(far, z)
    def body(n, carry):
        j = (far + n) % NZ

        @pl.when(j != z)
        def _():
            dcopy(far, j, 1 - c).wait_recv()
            frozen_chunk(far, j)
        return carry
    lax.fori_loop(1, NZ, body, 0)
    retire(LAST)
    dcopy(far, far, 1 - c).wait_recv()
    frozen_chunk(far, far)
    finish(far)

    def drain(ref, sem):
        pltpu.make_async_copy(ref, ref, sem).wait()

    drain(grads.at[pl.ds(0, 56)], zs)
    drain(grads.at[pl.ds(0, 64)], ds)
    for q in range(2):
        drain((fd, fu)[q].at[pl.ds(0, 30)], fs.at[q])
        drain(part_in.at[q], ps.at[q, 0])
        drain(rank_in.at[q], ps.at[q, 1])
        drain(acts.at[q, c, pl.ds(0, 7)], ps.at[q, 2])
        drain(acts.at[q, c], ps.at[q, 3])
        for h in range(2):
            drain(routes[h][1].at[q], ts.at[q, h, 0])
            drain(routes[h][3].at[q], ts.at[q, h, 1])


def on_device(inputs, output_gradient, weight, adapter_down, adapter_up, segment_adapter, adapter_slot_map):
    any_spec = pl.BlockSpec(memory_space=pl.ANY)
    smem = pl.BlockSpec(memory_space=pltpu.SMEM)
    vmem = pl.BlockSpec(memory_space=pltpu.VMEM)
    bf, f32 = jnp.bfloat16, jnp.float32
    dma = pltpu.SemaphoreType.DMA
    out, gd, gu = pl.pallas_call(
        kernel,
        out_shape=(
            jax.ShapeDtypeStruct((1024, 512), bf),
            jax.ShapeDtypeStruct((2, RANK, 512), f32),
            jax.ShapeDtypeStruct((2, RANK, 512), f32),
        ),
        in_specs=[smem, smem] + [any_spec] * 5,
        out_specs=(vmem, vmem, vmem),
        scratch_shapes=[
            pltpu.VMEM((128, 64, 1024), bf),
            pltpu.VMEM((NZ, 512, 1024), bf),
            pltpu.VMEM((1024, 512), bf),
            pltpu.VMEM((32, RANK, 512), bf),
            pltpu.VMEM((32, RANK, 512), bf),
            pltpu.VMEM((NZ, SEG, 512), f32),
            pltpu.VMEM((2, 2, NZ, HALF, SEG), f32),
            pltpu.VMEM((2, NZ, HALF, SEG), f32),
            pltpu.VMEM((2, NZ, HALF, SEG), f32),
            pltpu.VMEM((2, NZ - 1, HALF, SEG), f32),
            pltpu.VMEM((2, 2, NZ, HALF, SEG), bf),
            pltpu.VMEM((256, 1024), bf),
            pltpu.VMEM((2, 4, 8, HALF, 512), bf),
            pltpu.VMEM((2, 4, 8, HALF, 512), bf),
            pltpu.VMEM((2, 3, 8, HALF, 512), bf),
            pltpu.VMEM((2, 3, 8, HALF, 512), bf),
            pltpu.VMEM((2, 4, 2, HALF, 512), f32),
            pltpu.VMEM((2, 4, 2, HALF, 512), f32),
            pltpu.VMEM((2, 3, 2, HALF, 512), f32),
            pltpu.VMEM((2, 3, 2, HALF, 512), f32),
            dma((19,)),
            dma((64,)),
            dma((64,)),
            dma(()),
            dma(()),
            dma((2, 7)),
            dma((2,)),
            dma((2, 16)),
            dma((2, 4)),
            dma((2, 2, 6)),
            dma((2, 2, 2)),
        ],
        compiler_params=pltpu.CompilerParams(
            collective_id=0, has_side_effects=True, vmem_limit_bytes=60 * 1024 * 1024
        ),
    )(segment_adapter, adapter_slot_map, inputs, output_gradient, weight, adapter_down, adapter_up)
    return out, gd, gu


def solution(mesh):
    in_specs = (
        P("dp", "tensor"),
        P(("dp", "tensor"), None),
        P("tensor", None),
        P("dp", None, "tensor"),
        P("dp", None, "tensor"),
        P(),
        P(),
    )
    out_specs = (P("dp", "tensor"), P("dp", None, "tensor"), P("dp", None, "tensor"))
    return jax.shard_map(
        on_device, mesh=mesh, in_specs=in_specs, out_specs=out_specs, check_vma=False
    )
```

time: 276 us -> 125 us (0.45)
  waiting for transfers between devices: 153 us -> 0 us
  Pallas kernels: 0 us -> 118 us
  blocking collectives: 48.9 us -> 0 us
  matrix products: 29 us -> 0 us
  local copies, waits for them, and re-layouts: 20.5 us -> 5.6 us
  between operations: 14.2 us -> 0.64 us
  starting transfers between devices: 7.71 us -> 0 us
    pallas_call x0 -> x1, Pallas kernels: none -> 118 us  [on_device(): pl.pallas_call(kernel, out_shape=(jax.ShapeDtypeStruct((1024, 512), bf),...]
    reduce_scatter x1 -> x0, waiting for transfers between devices: 75.9 us -> none  [on_device(): lax.psum_scatter(full_table, 'dp', scatter_dimension=0, tiled=True)]
    all_to_all x1 -> x0, waiting for transfers between devices: 60.9 us -> none  [on_device(): lax.all_to_all(sending, 'dp', split_axis=0, concat_axis=0, tiled=True)]
    psum x1 -> x0, blocking collectives: 48.9 us -> none  [on_device(): down_acts, up_grads = lax.psum((down_part, up_part), 'tensor')]
    dot_general x9 -> x0, matrix products: 29 us -> none  [the longest x1 15.9 us: on_device(): lax.dot_general(full_grad, weight, (((1,), (1,)), ((), ())), preferred_el...]
    all_gather x1 -> x0, waiting for transfers between devices: 15.4 us -> none  [on_device(): full_grad = lax.all_gather(output_gradient, 'tensor', axis=0, tiled=True)]
    dot_general x1 -> x0, local copies, waits for them, and re-layouts: 8.08 us -> none  [on_device(): jnp.einsum('sa,scd->acd', onehot, seg_terms, precision=lax.Precision.HIGH...]
    all_to_all x1 -> x0, starting transfers between devices: 7.63 us -> none  [on_device(): lax.all_to_all(sending, 'dp', split_axis=0, concat_axis=0, tiled=True)]
  transfers between devices with their start and end apart: 3 -> 0, of which waited for: 3 -> 0; matrix products, arithmetic and copies ran while one was open for 12% -> 0% of each run, Pallas kernels for 0% -> 0%
where the time goes in v1:
time: 125 us; the launch traced here: 124 us
  Pallas kernels  118 us (94%)
  local copies, waits for them, and re-layouts  5.6 us (4%)
    pallas_call x1, Pallas kernels, on_device(): pl.pallas_call(kernel, out_shape=(jax.ShapeDtypeStruct((1024, 512), bf),...  118 us
    unnamed x3, local copies, waits for them, and re-layouts  5.6 us

profile of v1, /device:TPU:1, one launch (start us, length us, event | category | flops | bytes accessed | tf_op | source)
XLA Modules:
  0.0 124.4 jit_solution(9222715230974725720)
XLA Ops:
  0.6 118.1 %shard_map.94 = (bf16[1024,512]{1,0:T(8,128)(2,1)}, f32[2,64,512]{2,1,0:T(8,128)}, f32[2,64,512]{2,1,0:T(8,128)}) custom-call(s32[128]{0:T(128)} %seg_ref.1, s32[32]{0:T(128)} %map_ref.1, bf16[1024,512]{1,0:T(8,128)(2,1)} %x_hbm.1, bf16[64,8192]{1,0:T(8,128)(2,1)} %g_hbm.1, bf16[512,8192]{1,0:T(8,128)(2,1)} %w_hbm.1, bf16[2,64,512]{2,1,0:T(8,128)(2,1)} %fd_hbm.1, ...), custom_call_target="tpu_custom_call" | custom-call | tf_op jit(solution)/shard_map/pallas_call | solution.py:394
  118.8 2.3 %copy.13 = bf16[1024,512]{1,0:T(8,128)(2,1)} copy(bf16[1024,512]{1,0:T(8,128)(2,1)} %get-tuple-element.6) | data formatting | bytes 2097152
  121.0 1.7 %copy.14 = f32[2,64,512]{2,1,0:T(8,128)} copy(f32[2,64,512]{2,1,0:T(8,128)} %get-tuple-element.7) | data formatting | bytes 524288
  122.7 1.7 %copy.15 = f32[2,64,512]{2,1,0:T(8,128)} copy(f32[2,64,512]{2,1,0:T(8,128)} %get-tuple-element.8) | data formatting | bytes 524288

commit v2 on v1

--- a/solution.py
+++ b/solution.py
@@ -23,6 +23,22 @@
 LAST = len(ROUNDS) - 1
 
 
+def pairs():
+    waiting = {o: [(-1, 0)] for o in range(NZ)}
+    out = []
+    for k, (r, a) in enumerate(ROUNDS):
+        for way in (1,) if a == 3 and r in (0, 4) else (1, -1):
+            o = way * (r - a - 1) % NZ
+            waiting[o].append((k, -way * (a + 1) % NZ))
+            if len(waiting[o]) == 2:
+                out.append((k, o, waiting[o][0][1], waiting[o][1][1]))
+                waiting[o] = []
+    return out
+
+
+PAIRS = pairs()
+
+
 def dot(a, b, dims):
     return lax.dot_general(a, b, dims, preferred_element_type=jnp.float32)
 
@@ -32,7 +48,7 @@
     out_ref, gd_ref, gu_ref,
     grads, weight, acts_in, fd, fu, acc,
     part, part_in, chip_part, rank_in, acts, lhs,
-    tab0, tab1, tin0, tin1, sum0, sum1, sin0, sin1,
+    tab0, tab1, far0, far1, tin0, tin1, sum0, sum1, sfar0, sfar1, sin0, sin1,
     loc, zr, dr, zs, ds, fr, fs, pr, ps, tr, ts,
 ):
     dp = lax.axis_index("dp")
@@ -113,43 +129,91 @@
             zcopy(s, j, z + 1).wait_recv()
             dcopy(s, j, c).start()
 
-    def frozen(s, first, count, order):
-        def body(n, carry):
-            j = order(n)
-            dcopy(s, j, 1 - c).wait_recv()
-            g = grads[pl.ds((j * NZ + s) * 2, 2)].reshape(SEG, 1024)
-            acc[s] += dot(g, weight[j], NT)
-            return carry
-        lax.fori_loop(first, first + count, body, 0)
+    def frozen(o, first, second):
+        j, s0, s1 = (z + o) % NZ, (z + first) % NZ, (z + second) % NZ
+        dcopy(s0, j, 1 - c).wait_recv()
+        dcopy(s1, j, 1 - c).wait_recv()
+        g0 = grads[pl.ds((j * NZ + s0) * 2, 2)].reshape(SEG, 1024)
+        g1 = grads[pl.ds((j * NZ + s1) * 2, 2)].reshape(SEG, 1024)
+        t = dot(jnp.concatenate([g0, g1], axis=0), weight[j], NT)
+        acc[s0] += t[:SEG]
+        acc[s1] += t[SEG:]
 
     def slot_of(s):
         return map_ref[seg_ref[dp * NZ + s]]
 
-    def finish(s):
-        slot = slot_of(s)
-        act = acts[1, pl.ds(0, 2), s].reshape(RANK, SEG)
-        out = acc[s] + SCALE * dot(act, fd[slot], TN)
-        out_ref[pl.ds(pl.multiple_of(s * SEG, SEG), SEG), :] = out.astype(jnp.bfloat16)
+    def adapter_term():
+        def body(s, carry):
+            act = acts[1, pl.ds(0, 2), s].reshape(RANK, SEG)
+            acc[s] += SCALE * dot(act, fd[slot_of(s)], TN)
+            return carry
+        lax.fori_loop(0, NZ, body, 0)
+
+    def emit(s):
+        out_ref[pl.ds(pl.multiple_of(s * SEG, SEG), SEG), :] = acc[s].astype(jnp.bfloat16)
 
     kinds = ((fd, at_y, y, at_x, x), (fu, at_x, x, at_y, y))
 
-    def factors_first(q):
-        buf, at1, p1, _, p2 = kinds[q]
-        mine = pl.ds((p2 * 4 + p1) * 2, 2)
-        return [remote(buf.at[mine], buf.at[mine], fs.at[q], fr.at[q, d - 1], at1(p1 + d)) for d in (1, 2, 3)]
-
-    def factors_second(q):
-        buf, _, _, at2, p2 = kinds[q]
-        rows = pl.ds(p2 * 8, 8)
-        return [remote(buf.at[rows], buf.at[rows], fs.at[q], fr.at[q, 3], at2(p2 + 1)),
-                remote(buf.at[rows], buf.at[rows], fs.at[q], fr.at[q, 4], at2(p2 + 3))]
-
-    def factors_third(q):
-        buf, _, _, at2, p2 = kinds[q]
-        low = pl.ds(((p2 + 3) % 4) * 8, 4)
-        high = pl.ds(((p2 + 1) % 4) * 8 + 4, 4)
-        return [remote(buf.at[low], buf.at[low], fs.at[q], fr.at[q, 5], at2(p2 + 1)),
-                remote(buf.at[high], buf.at[high], fs.at[q], fr.at[q, 6], at2(p2 + 3))]
+    def fblock(q, row, col, first=0, count=2):
+        buf = kinds[q][0]
+        return buf.at[pl.ds((row % 4 * 4 + col % 4) * 2 + first, count)]
+
+    def fsend(q, block, sem, device):
+        return remote(block, block, fs.at[q], fr.at[q, sem], device)
+
+    def factors_own(q):
+        _, at1, p1, _, p2 = kinds[q]
+        mine = fblock(q, p2, p1)
+        return [fsend(q, mine, 0, at1(p1 + 1)), fsend(q, mine, 1, at1(p1 + 3))]
+
+    def factors_half(q):
+        _, at1, p1, _, p2 = kinds[q]
+        return [fsend(q, fblock(q, p2, p1 + 3, 0, 1), 2, at1(p1 + 1)),
+                fsend(q, fblock(q, p2, p1 + 1, 1, 1), 3, at1(p1 + 3))]
+
+    def factors_row(q, n):
+        _, _, p1, at2, p2 = kinds[q]
+        block = fblock(q, p2, p1 + (0, 3, 1, 2)[n])
+        return [fsend(q, block, 4 + n, at2(p2 + 1)), fsend(q, block, 8 + n, at2(p2 + 3))]
+
+    def factors_on(q, n):
+        _, _, p1, at2, p2 = kinds[q]
+        row, col, device = ((p2 + 3, p1, p2 + 1), (p2 + 3, p1 + 3, p2 + 1),
+                            (p2 + 1, p1 + 1, p2 + 3), (p2 + 1, p1 + 2, p2 + 3))[n]
+        return fsend(q, fblock(q, row, col), 12 + n, at2(device))
+
+    def fwait(q, *which):
+        for n in which:
+            half = n in (2, 3)
+            block = fblock(q, 0, 0, 0, 1 if half else 2)
+            fsend(q, block, n, partner).wait_recv()
+
+    def factors0():
+        for q in range(2):
+            start_all(factors_own(q) + factors_row(q, 0))
+
+    def factors1():
+        for q in range(2):
+            fwait(q, 0, 1)
+            start_all(factors_half(q) + factors_row(q, 1) + factors_row(q, 2))
+
+    def factors2():
+        for q in range(2):
+            fwait(q, 2, 3, 4)
+            start_all(factors_row(q, 3) + [factors_on(q, 0)])
+
+    def factors3():
+        for q in range(2):
+            fwait(q, 5, 10)
+            start_all([factors_on(q, 1), factors_on(q, 2)])
+
+    def factors4():
+        for q in range(2):
+            fwait(q, 11)
+            start_all([factors_on(q, 3)])
+
+    def factors5(q):
+        fwait(q, 6, 7, 8, 9, 12, 13, 14, 15)
 
     def start_all(copies):
         for cp in copies:
@@ -210,13 +274,15 @@
         acts[q, c, z] = t.astype(jnp.bfloat16)
         start_all(share_acts(q))
 
-    routes = ((tab0, tin0, sum0, sin0, at_x, x, at_y, y), (tab1, tin1, sum1, sin1, at_y, y, at_x, x))
+    routes = ((tab0, far0, tin0, sum0, sfar0, sin0, at_x, x, at_y, y),
+              (tab1, far1, tin1, sum1, sfar1, sin1, at_y, y, at_x, x))
 
     def table(q):
         for h in range(2):
-            tab = routes[h][0]
-
-            def body(g, carry):
+            tab, p1 = routes[h][0], routes[h][7]
+
+            def body(n, carry):
+                g = (p1 + 2 + 3 * n) % 4
                 for s in range(NZ):
                     slot = slot_of(s)
                     v = acts[q, h, s]
@@ -231,43 +297,76 @@
                     rhs = acts_in[...]
                 t = dot(lhs[...], rhs, NN) * (SCALE / SEG)
                 tab[q, g] = t.astype(jnp.bfloat16).reshape(8, HALF, 512)
+
+                @pl.when(n == 0)
+                def _():
+                    start_all(table_a(q, h))
                 return carry
             lax.fori_loop(0, 4, body, 0)
-            start_all(table_first(q, h))
-
-    def table_first(q, h):
-        tab, tin, _, _, at1, p1, _, _ = routes[h]
-        return [remote(tab.at[q, (p1 + d) % 4], tin.at[q, d - 1], ts.at[q, h, 0], tr.at[q, h, d - 1], at1(p1 + d))
-                for d in (1, 2, 3)]
-
-    def table_second(q, h):
-        _, _, total, sin, _, _, at2, p2 = routes[h]
-        return [remote(total.at[q, (p2 + d) % 4], sin.at[q, d - 1], ts.at[q, h, 1], tr.at[q, h, 2 + d], at2(p2 + d))
-                for d in (1, 2, 3)]
-
-    def table_sum(q):
+
+    def table_a(q, h):
+        tab, far, _, _, _, _, at1, p1, _, _ = routes[h]
+        g = (p1 + 2) % 4
+        return [remote(tab.at[q, g, pl.ds(0, 4)], far.at[q, 0], ts.at[q, h, 0], tr.at[q, h, 0], at1(p1 + 1)),
+                remote(tab.at[q, g, pl.ds(4, 4)], far.at[q, 1], ts.at[q, h, 0], tr.at[q, h, 1], at1(p1 + 3))]
+
+    def table_b(q, h):
+        tab, _, tin, _, _, _, at1, p1, _, _ = routes[h]
+        return [remote(tab.at[q, (p1 + 1) % 4], tin.at[q, 0], ts.at[q, h, 0], tr.at[q, h, 2], at1(p1 + 1)),
+                remote(tab.at[q, (p1 + 3) % 4], tin.at[q, 1], ts.at[q, h, 0], tr.at[q, h, 3], at1(p1 + 3))]
+
+    def table_c(q, h):
+        _, _, _, total, sfar, _, _, _, at2, p2 = routes[h]
+        g = (p2 + 2) % 4
+        return [remote(total.at[q, g, 0], sfar.at[q, 0], ts.at[q, h, 1], tr.at[q, h, 4], at2(p2 + 1)),
+                remote(total.at[q, g, 1], sfar.at[q, 1], ts.at[q, h, 1], tr.at[q, h, 5], at2(p2 + 3))]
+
+    def table_d(q, h):
+        _, _, _, total, _, sin, _, _, at2, p2 = routes[h]
+        return [remote(total.at[q, (p2 + 1) % 4], sin.at[q, 0], ts.at[q, h, 1], tr.at[q, h, 6], at2(p2 + 1)),
+                remote(total.at[q, (p2 + 3) % 4], sin.at[q, 1], ts.at[q, h, 1], tr.at[q, h, 7], at2(p2 + 3))]
+
+    def pass_on(q):
         for h in range(2):
-            tab, tin, total, _, _, p1, _, _ = routes[h]
-            await_all(table_first(q, h))
+            tab, far, p1 = routes[h][0], routes[h][1], routes[h][7]
+            send_a, send_b = table_a(q, h), table_b(q, h)
+            for way in range(2):
+                send_a[way].wait_recv()
+                g, half = (p1 + (1, 3)[way]) % 4, pl.ds(way * 4, 4)
+                t = tab[q, g, half].astype(jnp.float32) + far[q, way].astype(jnp.float32)
+                tab[q, g, half] = t.astype(jnp.bfloat16)
+                send_b[way].start()
+
+    def turn(q):
+        for h in range(2):
+            tab, tin, total, p1, p2 = routes[h][0], routes[h][2], routes[h][3], routes[h][7], routes[h][9]
+            await_all(table_b(q, h))
 
             def body(n, carry):
-                t = tab[q, p1, pl.ds(n * 2, 2)].astype(jnp.float32)
-                for d in range(3):
-                    t = t + tin[q, d, pl.ds(n * 2, 2)].astype(jnp.float32)
-                total[q, n] = t
+                g = (p2 + 2 + n) % 4
+                rows = pl.ds(g * 2, 2)
+                t = tab[q, p1, rows].astype(jnp.float32) + tin[q, 0, rows].astype(jnp.float32)
+                total[q, g] = t + tin[q, 1, rows].astype(jnp.float32)
                 return carry
             lax.fori_loop(0, 4, body, 0)
-            start_all(table_second(q, h))
+            start_all(table_c(q, h))
+
+    def pass_sum(q):
+        for h in range(2):
+            total, sfar, p2 = routes[h][3], routes[h][4], routes[h][9]
+            send_c, send_d = table_c(q, h), table_d(q, h)
+            for way in range(2):
+                send_c[way].wait_recv()
+                g = (p2 + (1, 3)[way]) % 4
+                total[q, g, way] += sfar[q, way]
+                send_d[way].start()
 
     def table_end(q):
         ref = (gu_ref, gd_ref)[q]
         for h in range(2):
-            _, _, total, sin, _, _, _, p2 = routes[h]
-            await_all(table_second(q, h))
-            t = total[q, p2]
-            for d in range(3):
-                t = t + sin[q, d]
-            ref[:, h * HALF:(h + 1) * HALF, :] = t
+            total, sin, p2 = routes[h][3], routes[h][5], routes[h][9]
+            await_all(table_d(q, h))
+            ref[:, h * HALF:(h + 1) * HALF, :] = total[q, p2] + sin[q, 0] + sin[q, 1]
 
     def start_own():
         for j in range(NZ):
@@ -281,93 +380,75 @@
         for cp in load_w:
             cp.wait()
 
-    def forward(s):
-        return lambda n: (s + n) % NZ
-
-    def whole(s):
-        frozen(s, 0, NZ, forward(s))
-
     def near(a, way):
         return (z + way * a + NZ) % NZ
 
+    retired, consumed, emitted = [0], [0], []
+
+    def last_use(d):
+        return max(k for k, _, s0, s1 in PAIRS if d in (s0, s1))
+
+    def retire_to(k):
+        while retired[0] <= k:
+            retire(retired[0])
+            retired[0] += 1
+
+    def consume_to(k):
+        retire_to(k)
+        while consumed[0] < len(PAIRS) and PAIRS[consumed[0]][0] <= k:
+            frozen(*PAIRS[consumed[0]][1:])
+            consumed[0] += 1
+
     hooks = {
-        0: [lambda: own_fd.wait(), lambda: own_fu.wait(), lambda: start_all(factors_first(0)),
-            lambda: start_all(factors_first(1)), start_own],
+        0: [own_fd.wait, own_fu.wait, factors0, start_own],
         1: [zero],
-        2: [lambda: await_all(factors_first(0)), lambda: await_all(factors_first(1)),
-            lambda: start_all(factors_second(0)), lambda: start_all(factors_second(1))],
-        3: [loads_done, lambda: whole(z)],
-        6: [lambda: await_all(factors_second(0)), lambda: await_all(factors_second(1)),
-            lambda: start_all(factors_third(0)), lambda: start_all(factors_third(1))],
-        9: [lambda: await_all(factors_third(0)), lambda: project(0), lambda: share_core(0).start()],
-        10: [lambda: await_all(factors_third(1)), lambda: reduce_core(0)],
-        12: [lambda: own_cols_ready(), lambda: project(1), lambda: share_core(1).start(),
-             lambda: reduce_chips(0)],
-        13: [lambda: reduce_core(1)],
-        14: [lambda: await_acts(0), lambda: cross_acts(0).start()],
-        15: [lambda: await_cross(0), lambda: table(0), lambda: reduce_chips(1)],
-        17: [lambda: await_acts(1), lambda: cross_acts(1).start(), lambda: frozen_rest(near(1, -1))],
-        18: [lambda: await_cross(1), lambda: table(1)],
-        19: [lambda: frozen_rest(near(1, 1))],
-        20: [lambda: table_sum(0)],
-        21: [lambda: finish(z), lambda: finish(near(1, -1)), lambda: finish(near(1, 1))],
-        22: [lambda: frozen_rest(near(2, -1))],
-        23: [lambda: frozen_rest(near(2, 1))],
-        24: [lambda: table_end(0), lambda: table_sum(1)],
-        25: [lambda: finish(near(2, -1)), lambda: finish(near(2, 1))],
-        28: [lambda: frozen_rest(near(3, -1)), lambda: frozen_rest(near(3, 1)),
-             lambda: finish(near(3, -1)), lambda: finish(near(3, 1)), lambda: table_end(1)],
+        2: [loads_done],
+        3: [factors1],
+        5: [factors2],
+        7: [factors3],
+        8: [factors4],
+        9: [lambda: factors5(0)],
+        10: [lambda: project(0), lambda: share_core(0).start(), lambda: factors5(1)],
+        11: [lambda: reduce_core(0), lambda: consume_to(9), lambda: project(1), lambda: share_core(1).start()],
+        12: [lambda: reduce_core(1)],
+        14: [lambda: reduce_chips(0)],
+        15: [lambda: reduce_chips(1)],
+        17: [lambda: await_acts(0), lambda: cross_acts(0).start()],
+        18: [lambda: await_acts(1), lambda: cross_acts(1).start(), lambda: await_cross(0), lambda: table(0)],
+        19: [lambda: await_cross(1), lambda: table(1)],
+        20: [lambda: pass_on(0), adapter_term],
+        21: [lambda: pass_on(1), lambda: None],
+        23: [lambda: turn(0), lambda: None],
+        24: [lambda: turn(1)],
+        25: [lambda: pass_sum(0)],
+        26: [lambda: pass_sum(1)],
+        27: [lambda: table_end(0)],
+        28: [lambda: table_end(1)],
     }
-
-    def own_cols_ready():
-        def body(n, carry):
-            dcopy((z + n) % NZ, z, 1 - c).wait_recv()
-            return carry
-        lax.fori_loop(1, NZ, body, 0)
-
-    def frozen_chunk(s, j):
-        g = grads[pl.ds((j * NZ + s) * 2, 2)].reshape(SEG, 1024)
-        acc[s] += dot(g, weight[j], NT)
-
-    def frozen_rest(s):
-        def body(n, carry):
-            j = (z + n) % NZ
-            dcopy(s, j, 1 - c).wait_recv()
-            frozen_chunk(s, j)
-            return carry
-        frozen_chunk(s, z)
-        lax.fori_loop(1, NZ, body, 0)
 
     for cp in own:
         cp.wait()
-    done = 0
     for k in range(len(ROUNDS)):
-        lag = 2 if k < len(FIRST) + 2 else 3
-        while done <= k - lag:
-            retire(done)
-            done += 1
+        lag = 2 if k < 17 else 3
+        retire_to(k - lag)
         issue(k)
+        consume_to(k - lag - 1)
         for hook in hooks.get(k, []):
             hook()
-    far = near(4, 1)
-    while done < LAST:
-        retire(done)
-        done += 1
-
-    frozen_chunk(far, z)
-    def body(n, carry):
-        j = (far + n) % NZ
-
-        @pl.when(j != z)
-        def _():
-            dcopy(far, j, 1 - c).wait_recv()
-            frozen_chunk(far, j)
-        return carry
-    lax.fori_loop(1, NZ, body, 0)
-    retire(LAST)
-    dcopy(far, far, 1 - c).wait_recv()
-    frozen_chunk(far, far)
-    finish(far)
+    retire_to(LAST - 2)
+    consume_to(LAST - 4)
+    for d in (0, 1, 2):
+        for way in (1,) if d == 0 else (1, -1):
+            if last_use(way * d % NZ) <= LAST - 4:
+                emit((z + way * d + NZ) % NZ)
+                emitted.append(way * d % NZ)
+    retire_to(LAST - 1)
+    consume_to(LAST - 2)
+    retire_to(LAST)
+    consume_to(LAST)
+    for d in range(NZ):
+        if d not in emitted:
+            emit((z + d) % NZ)
 
     def drain(ref, sem):
         pltpu.make_async_copy(ref, ref, sem).wait()
@@ -381,8 +462,16 @@
         drain(acts.at[q, c, pl.ds(0, 7)], ps.at[q, 2])
         drain(acts.at[q, c], ps.at[q, 3])
         for h in range(2):
-            drain(routes[h][1].at[q], ts.at[q, h, 0])
-            drain(routes[h][3].at[q], ts.at[q, h, 1])
+            drain(routes[h][0].at[q, pl.ds(0, 3)], ts.at[q, h, 0])
+            drain(routes[h][3].at[q, pl.ds(0, 3)], ts.at[q, h, 1])
+
+
+def store(*refs):
+    copies = [pltpu.make_async_copy(refs[i], refs[3 + i], refs[6].at[i]) for i in range(3)]
+    for cp in copies:
+        cp.start()
+    for cp in copies:
+        cp.wait()
 
 
 def on_device(inputs, output_gradient, weight, adapter_down, adapter_up, segment_adapter, adapter_slot_map):
@@ -394,9 +483,9 @@
     out, gd, gu = pl.pallas_call(
         kernel,
         out_shape=(
-            jax.ShapeDtypeStruct((1024, 512), bf),
-            jax.ShapeDtypeStruct((2, RANK, 512), f32),
-            jax.ShapeDtypeStruct((2, RANK, 512), f32),
+            pltpu.VMEM((1024, 512), bf),
+            pltpu.VMEM((2, RANK, 512), f32),
+            pltpu.VMEM((2, RANK, 512), f32),
         ),
         in_specs=[smem, smem] + [any_spec] * 5,
         out_specs=(vmem, vmem, vmem),
@@ -415,29 +504,43 @@
             pltpu.VMEM((256, 1024), bf),
             pltpu.VMEM((2, 4, 8, HALF, 512), bf),
             pltpu.VMEM((2, 4, 8, HALF, 512), bf),
-            pltpu.VMEM((2, 3, 8, HALF, 512), bf),
-            pltpu.VMEM((2, 3, 8, HALF, 512), bf),
+            pltpu.VMEM((2, 2, 4, HALF, 512), bf),
+            pltpu.VMEM((2, 2, 4, HALF, 512), bf),
+            pltpu.VMEM((2, 2, 8, HALF, 512), bf),
+            pltpu.VMEM((2, 2, 8, HALF, 512), bf),
             pltpu.VMEM((2, 4, 2, HALF, 512), f32),
             pltpu.VMEM((2, 4, 2, HALF, 512), f32),
-            pltpu.VMEM((2, 3, 2, HALF, 512), f32),
-            pltpu.VMEM((2, 3, 2, HALF, 512), f32),
+            pltpu.VMEM((2, 2, HALF, 512), f32),
+            pltpu.VMEM((2, 2, HALF, 512), f32),
+            pltpu.VMEM((2, 2, 2, HALF, 512), f32),
+            pltpu.VMEM((2, 2, 2, HALF, 512), f32),
             dma((19,)),
             dma((64,)),
             dma((64,)),
             dma(()),
             dma(()),
-            dma((2, 7)),
+            dma((2, 16)),
             dma((2,)),
             dma((2, 16)),
             dma((2, 4)),
-            dma((2, 2, 6)),
+            dma((2, 2, 8)),
             dma((2, 2, 2)),
         ],
         compiler_params=pltpu.CompilerParams(
-            collective_id=0, has_side_effects=True, vmem_limit_bytes=60 * 1024 * 1024
+            collective_id=0, has_side_effects=True, vmem_limit_bytes=56 * 1024 * 1024
         ),
     )(segment_adapter, adapter_slot_map, inputs, output_gradient, weight, adapter_down, adapter_up)
-    return out, gd, gu
+    return pl.pallas_call(
+        store,
+        out_shape=(
+            jax.ShapeDtypeStruct((1024, 512), bf),
+            jax.ShapeDtypeStruct((2, RANK, 512), f32),
+            jax.ShapeDtypeStruct((2, RANK, 512), f32),
+        ),
+        in_specs=[vmem] * 3,
+        out_specs=(any_spec,) * 3,
+        scratch_shapes=[dma((3,))],
+    )(*(pltpu.with_memory_space_constraint(o, pltpu.VMEM) for o in (out, gd, gu)))
 
 
 def solution(mesh):

time: 125 us -> 111 us (0.89)
  Pallas kernels: 118 us -> 110 us
  local copies, waits for them, and re-layouts: 5.6 us -> 0 us
    pallas_call x1 -> x2, Pallas kernels: 118 us -> 110 us  [the longest x1 109 us: on_device(): pl.pallas_call(kernel, out_shape=(pltpu.VMEM((1024, 512), bf), pltpu.VMEM...]
    unnamed x3 -> x0, local copies, waits for them, and re-layouts: 5.6 us -> none
where the time goes in v2:
time: 111 us
  Pallas kernels  110 us (99%)
    pallas_call x1, Pallas kernels, on_device(): pl.pallas_call(kernel, out_shape=(pltpu.VMEM((1024, 512), bf), pltpu.VMEM...  109 us

profile of v2, /device:TPU:1, one launch (start us, length us, event | category | flops | bytes accessed | tf_op | source)
XLA Modules:
  0.0 110.5 jit_solution(16141404789837938343)
XLA Ops:
  0.6 108.6 %shard_map.94 = (bf16[1024,512]{1,0:T(8,128)(2,1)S(1)}, f32[2,64,512]{2,1,0:T(8,128)S(1)}, f32[2,64,512]{2,1,0:T(8,128)S(1)}) custom-call(s32[128]{0:T(128)} %seg_ref.1, s32[32]{0:T(128)} %map_ref.1, bf16[1024,512]{1,0:T(8,128)(2,1)} %x_hbm.1, bf16[64,8192]{1,0:T(8,128)(2,1)} %g_hbm.1, bf16[512,8192]{1,0:T(8,128)(2,1)} %w_hbm.1, bf16[2,64,512]{2,1,0:T(8,128)(2,1)} %fd_hbm.1, ...), custom_call_target="tpu_custom_call" | custom-call | tf_op jit(solution)/shard_map/pallas_call | solution.py:483
  109.2 1.2 %shard_map.95 = (bf16[1024,512]{1,0:T(8,128)(2,1)}, f32[2,64,512]{2,1,0:T(8,128)}, f32[2,64,512]{2,1,0:T(8,128)}) custom-call(bf16[1024,512]{1,0:T(8,128)(2,1)S(1)} %get-tuple-element.6.refs_0_, f32[2,64,512]{2,1,0:T(8,128)S(1)} %get-tuple-element.7.refs_1_, f32[2,64,512]{2,1,0:T(8,128)S(1)} %get-tuple-element.8.refs_2_), custom_call_target="tpu_custom_call" | custom-call | tf_op jit(solution)/shard_map/pallas_call | solution.py:533

commit v3 on v2

--- a/solution.py
+++ b/solution.py
@@ -89,16 +89,26 @@
     barrier = pltpu.get_barrier_semaphore()
     for d in range(1, NZ):
         pl.semaphore_signal(barrier, inc=1, device_id=at_z(z + d), device_id_type=MESH)
-    for d in range(1, 4):
+    for d in (1, 3):
         pl.semaphore_signal(barrier, inc=1, device_id=at_x(x + d), device_id_type=MESH)
         pl.semaphore_signal(barrier, inc=1, device_id=at_y(y + d), device_id_type=MESH)
     pl.semaphore_signal(barrier, inc=1, device_id=partner, device_id_type=MESH)
-    pl.semaphore_wait(barrier, 14)
+    pl.semaphore_wait(barrier, 12)
 
     def zcopy(s, j, zz):
         i = (j * NZ + s) * 2 + c
         return remote(grads.at[i], grads.at[i], zs, zr.at[j * NZ + s], at_z(zz))
 
+    def last_z(half, way):
+        s, j = chunk(way, *ROUNDS[LAST])
+        ref = grads.at[(j * NZ + s) * 2 + c, :, pl.ds(half * 512, 512)]
+        return remote(ref, ref, zs, zr.at[64 + half], at_z(z + NZ + way))
+
+    def last_d(half, core):
+        far = (z + 4) % NZ
+        ref = grads.at[(far * NZ + far) * 2 + core, :, pl.ds(half * 512, 512)]
+        return remote(ref, ref, ds, dr.at[64 + half], partner)
+
     def dcopy(s, j, core):
         i = (j * NZ + s) * 2 + core
         return remote(grads.at[i], grads.at[i], ds, dr.at[j * NZ + s], partner)
@@ -109,7 +119,13 @@
 
     def issue(k):
         r, a = ROUNDS[k]
-        if a == 3 and r in (0, 4):
+        if k == LAST:
+            for core, way in ((0, 1), (1, -1)):
+                @pl.when(c == core)
+                def _():
+                    last_z(0, way).start()
+                    last_z(1, way).start()
+        elif a == 3 and r in (0, 4):
             @pl.when(c == 0)
             def _():
                 zcopy(*chunk(1, r, a), z + 1).start()
@@ -411,25 +427,23 @@
         10: [lambda: project(0), lambda: share_core(0).start(), lambda: factors5(1)],
         11: [lambda: reduce_core(0), lambda: consume_to(9), lambda: project(1), lambda: share_core(1).start()],
         12: [lambda: reduce_core(1)],
-        14: [lambda: reduce_chips(0)],
-        15: [lambda: reduce_chips(1)],
-        17: [lambda: await_acts(0), lambda: cross_acts(0).start()],
-        18: [lambda: await_acts(1), lambda: cross_acts(1).start(), lambda: await_cross(0), lambda: table(0)],
+        13: [lambda: reduce_chips(0)],
+        15: [lambda: await_acts(0), lambda: cross_acts(0).start(), lambda: reduce_chips(1)],
+        16: [lambda: await_cross(0), lambda: table(0)],
+        18: [lambda: await_acts(1), lambda: cross_acts(1).start(), lambda: pass_on(0)],
         19: [lambda: await_cross(1), lambda: table(1)],
-        20: [lambda: pass_on(0), adapter_term],
-        21: [lambda: pass_on(1), lambda: None],
-        23: [lambda: turn(0), lambda: None],
+        20: [adapter_term],
+        21: [lambda: pass_on(1), lambda: turn(0)],
+        23: [lambda: pass_sum(0)],
         24: [lambda: turn(1)],
-        25: [lambda: pass_sum(0)],
+        25: [lambda: table_end(0)],
         26: [lambda: pass_sum(1)],
-        27: [lambda: table_end(0)],
-        28: [lambda: table_end(1)],
     }
 
     for cp in own:
         cp.wait()
     for k in range(len(ROUNDS)):
-        lag = 2 if k < 17 else 3
+        lag = 2 if k < 10 else 3
         retire_to(k - lag)
         issue(k)
         consume_to(k - lag - 1)
@@ -444,11 +458,28 @@
                 emitted.append(way * d % NZ)
     retire_to(LAST - 1)
     consume_to(LAST - 2)
-    retire_to(LAST)
-    consume_to(LAST)
+    far, others = near(4, 1), PAIRS[-1]
+    for half in range(2):
+        last_z(half, 1).wait_recv()
+        last_d(half, c).start()
+    consume_to(LAST - 1)
     for d in range(NZ):
-        if d not in emitted:
-            emit((z + d) % NZ)
+        if d not in emitted and d != 4:
+            if d != others[2]:
+                emit((z + d) % NZ)
+    other = (z + others[2]) % NZ
+    table_end(1)
+    dcopy(other, far, 1 - c).wait_recv()
+    for half in range(2):
+        last_d(half, 1 - c).wait_recv()
+        cols = pl.ds(half * 512, 512)
+        g0 = grads[pl.ds((far * NZ + other) * 2, 2), :, cols].reshape(SEG, 512)
+        g1 = grads[pl.ds((far * NZ + far) * 2, 2), :, cols].reshape(SEG, 512)
+        t = dot(jnp.concatenate([g0, g1], axis=0), weight[far, :, cols], NT)
+        acc[other] += t[:SEG]
+        acc[far] += t[SEG:]
+    emit(other)
+    emit(far)
 
     def drain(ref, sem):
         pltpu.make_async_copy(ref, ref, sem).wait()
@@ -515,8 +546,8 @@
             pltpu.VMEM((2, 2, 2, HALF, 512), f32),
             pltpu.VMEM((2, 2, 2, HALF, 512), f32),
             dma((19,)),
-            dma((64,)),
-            dma((64,)),
+            dma((66,)),
+            dma((66,)),
             dma(()),
             dma(()),
             dma((2, 16)),

time: 111 us -> 110 us (level)
  no operation moved by 1% of the time
where the time goes in v3:
time: 110 us
  Pallas kernels  109 us (99%)
    pallas_call x1, Pallas kernels, on_device(): pl.pallas_call(kernel, out_shape=(pltpu.VMEM((1024, 512), bf), pltpu.VMEM...  108 us

profile of v3, /device:TPU:1, one launch (start us, length us, event | category | flops | bytes accessed | tf_op | source)
XLA Modules:
  0.0 109.6 jit_solution(9828938797722881546)
XLA Ops:
  0.6 107.7 %shard_map.94 = (bf16[1024,512]{1,0:T(8,128)(2,1)S(1)}, f32[2,64,512]{2,1,0:T(8,128)S(1)}, f32[2,64,512]{2,1,0:T(8,128)S(1)}) custom-call(s32[128]{0:T(128)} %seg_ref.1, s32[32]{0:T(128)} %map_ref.1, bf16[1024,512]{1,0:T(8,128)(2,1)} %x_hbm.1, bf16[64,8192]{1,0:T(8,128)(2,1)} %g_hbm.1, bf16[512,8192]{1,0:T(8,128)(2,1)} %w_hbm.1, bf16[2,64,512]{2,1,0:T(8,128)(2,1)} %fd_hbm.1, ...), custom_call_target="tpu_custom_call" | custom-call | tf_op jit(solution)/shard_map/pallas_call | solution.py:514
  108.3 1.2 %shard_map.95 = (bf16[1024,512]{1,0:T(8,128)(2,1)}, f32[2,64,512]{2,1,0:T(8,128)}, f32[2,64,512]{2,1,0:T(8,128)}) custom-call(bf16[1024,512]{1,0:T(8,128)(2,1)S(1)} %get-tuple-element.6.refs_0_, f32[2,64,512]{2,1,0:T(8,128)S(1)} %get-tuple-element.7.refs_1_, f32[2,64,512]{2,1,0:T(8,128)S(1)} %get-tuple-element.8.refs_2_), custom_call_target="tpu_custom_call" | custom-call | tf_op jit(solution)/shard_map/pallas_call | solution.py:564

commit v4 on v3

--- a/solution.py
+++ b/solution.py
@@ -72,10 +72,19 @@
             device_id=device, device_id_type=MESH,
         )
 
+    barrier = pltpu.get_barrier_semaphore()
+    for d in range(1, NZ):
+        pl.semaphore_signal(barrier, inc=1, device_id=at_z(z + d), device_id_type=MESH)
+    for d in (1, 3):
+        pl.semaphore_signal(barrier, inc=1, device_id=at_x(x + d), device_id_type=MESH)
+        pl.semaphore_signal(barrier, inc=1, device_id=at_y(y + d), device_id_type=MESH)
+    pl.semaphore_signal(barrier, inc=1, device_id=partner, device_id_type=MESH)
+
     own = []
-    for j in range(NZ):
-        own.append(pltpu.make_async_copy(
-            g_hbm.at[:, pl.ds(j * 1024, 1024)], grads.at[(j * NZ + z) * 2 + c], loc.at[j]))
+    for n, o in enumerate((4, 3, 5, 2, 6, 1, 7, 0)):
+        j = (z + o) % NZ
+        cols = pl.ds(pl.multiple_of(j * 1024, 1024), 1024)
+        own.append(pltpu.make_async_copy(g_hbm.at[:, cols], grads.at[(j * NZ + z) * 2 + c], loc.at[n]))
     own_fd = pltpu.make_async_copy(fd_hbm, fd.at[pl.ds((x * 4 + y) * 2, 2)], loc.at[8])
     own_fu = pltpu.make_async_copy(fu_hbm, fu.at[pl.ds((y * 4 + x) * 2, 2)], loc.at[9])
     load_x = pltpu.make_async_copy(x_hbm, acts_in, loc.at[10])
@@ -83,16 +92,9 @@
         pltpu.make_async_copy(w_hbm.at[:, pl.ds(j * 1024, 1024)], weight.at[j], loc.at[11 + j])
         for j in range(NZ)
     ]
-    for cp in own + [own_fd, own_fu, load_x] + load_w:
+    for cp in own + [own_fd, own_fu]:
         cp.start()
 
-    barrier = pltpu.get_barrier_semaphore()
-    for d in range(1, NZ):
-        pl.semaphore_signal(barrier, inc=1, device_id=at_z(z + d), device_id_type=MESH)
-    for d in (1, 3):
-        pl.semaphore_signal(barrier, inc=1, device_id=at_x(x + d), device_id_type=MESH)
-        pl.semaphore_signal(barrier, inc=1, device_id=at_y(y + d), device_id_type=MESH)
-    pl.semaphore_signal(barrier, inc=1, device_id=partner, device_id_type=MESH)
     pl.semaphore_wait(barrier, 12)
 
     def zcopy(s, j, zz):
@@ -415,9 +417,13 @@
             frozen(*PAIRS[consumed[0]][1:])
             consumed[0] += 1
 
+    def rest_own():
+        for cp in own[3:]:
+            cp.wait()
+
     hooks = {
-        0: [own_fd.wait, own_fu.wait, factors0, start_own],
-        1: [zero],
+        0: [own_fd.wait, own_fu.wait, factors0, own[1].wait, own[2].wait],
+        1: [lambda: start_all([load_x] + load_w), rest_own, start_own, zero],
         2: [loads_done],
         3: [factors1],
         5: [factors2],
@@ -440,8 +446,7 @@
         26: [lambda: pass_sum(1)],
     }
 
-    for cp in own:
-        cp.wait()
+    own[0].wait()
     for k in range(len(ROUNDS)):
         lag = 2 if k < 10 else 3
         retire_to(k - lag)

time: 110 us -> 110 us (level)
  no operation moved by 1% of the time
where the time goes in v4:
time: 110 us
  Pallas kernels  109 us (99%)
    pallas_call x1, Pallas kernels, on_device(): pl.pallas_call(kernel, out_shape=(pltpu.VMEM((1024, 512), bf), pltpu.VMEM...  108 us

profile of v4, /device:TPU:1, one launch (start us, length us, event | category | flops | bytes accessed | tf_op | source)
XLA Modules:
  0.0 109.7 jit_solution(18170207031690175810)
XLA Ops:
  0.6 107.8 %shard_map.94 = (bf16[1024,512]{1,0:T(8,128)(2,1)S(1)}, f32[2,64,512]{2,1,0:T(8,128)S(1)}, f32[2,64,512]{2,1,0:T(8,128)S(1)}) custom-call(s32[128]{0:T(128)} %seg_ref.1, s32[32]{0:T(128)} %map_ref.1, bf16[1024,512]{1,0:T(8,128)(2,1)} %x_hbm.1, bf16[64,8192]{1,0:T(8,128)(2,1)} %g_hbm.1, bf16[512,8192]{1,0:T(8,128)(2,1)} %w_hbm.1, bf16[2,64,512]{2,1,0:T(8,128)(2,1)} %fd_hbm.1, ...), custom_call_target="tpu_custom_call" | custom-call | tf_op jit(solution)/shard_map/pallas_call | solution.py:519
  108.4 1.2 %shard_map.95 = (bf16[1024,512]{1,0:T(8,128)(2,1)}, f32[2,64,512]{2,1,0:T(8,128)}, f32[2,64,512]{2,1,0:T(8,128)}) custom-call(bf16[1024,512]{1,0:T(8,128)(2,1)S(1)} %get-tuple-element.6.refs_0_, f32[2,64,512]{2,1,0:T(8,128)S(1)} %get-tuple-element.7.refs_1_, f32[2,64,512]{2,1,0:T(8,128)S(1)} %get-tuple-element.8.refs_2_), custom_call_target="tpu_custom_call" | custom-call | tf_op jit(solution)/shard_map/pallas_call | solution.py:569
